TPU v7x, 32 devices: a whole 2x2x4 slice. The times are simulated.
32 devices in a mesh: stripe: 2 (over x), tile: 16 (over z, y, core).
Axes of the slice: x: 2, y: 2, z: 4, core: 2. Of those that a mesh axis runs over, the one named last changes fastest.
Arguments:
- mask_tiles: float32 [32, 1024, 1024], P(('stripe', 'tile')), parts along dimension 0, may hold values from -1 to 1
- target_grid: float32 [32, 16384], P(('stripe', 'tile')), parts along dimension 0, may hold values from 0 to 1
- kernels: float32 [16, 2, 24, 64, 96], P('tile'), may hold values from -48 to 48
- kern_weight: float32 [24], replicated, may hold values from 0.05 to 1
- owner_list: int32 [32, 1], P('stripe'), parts along dimension 0, may hold values from 0 to 15, as said below
Outputs:
- mask_out: float32 [32, 1024, 1024], P(('stripe', 'tile')), parts along dimension 0
- owner_error: float32 [32], P(('stripe', 'tile')), parts along dimension 0
There are 2 independent parts, one for each index of `stripe`. A program takes and returns all parts, laid end to end along the dimension named above; an argument that names none is the same for every part. Nothing has to cross between parts.
Inputs may be any that keep to these rules, and one draw needn't show every extreme that they name: `owner_list`: every owner is named by 0 to 2 tiles of a stripe, and some owner by exactly 2.
All inputs are finite; a program needn't handle non-finite values.
Results may differ from a plain program's by a relative error of at most 0.0001.
Values sent between devices are 32-bit elements; how exact they have to be, the bound alone decides.
A program may use at most 128 MiB of HBM per device.

v0:
```python
import functools

import jax
import jax.numpy as jnp
import ml_dtypes
import numpy as np
from jax import lax
from jax.experimental import pallas as pl
from jax.experimental.pallas import tpu as pltpu
from jax.sharding import PartitionSpec as P

AMBIT = 256
DIFF_STEPS = 2
GRID_X = 192
GRID_Y = 128
CORE_X = 128
MOST = 2
ROWS = 80
LANES = 128

RESIST_SLOPE = 3.0
RESIST_LEVEL = 1.2
DIFFUSE_RATE = 0.2
STEP_SIZE = 1.0

F32 = jnp.float32
BF16 = jnp.bfloat16
HIGHEST = lax.Precision.HIGHEST


def angle(length, positions, freqs):
    turns = np.mod(np.outer(positions, freqs), length).astype(np.float64) / length
    return 2.0 * np.pi * turns


def halves(table):
    high = table.astype(np.float32).astype(ml_dtypes.bfloat16)
    low = (table - high.astype(np.float64)).astype(np.float32).astype(ml_dtypes.bfloat16)
    return high, low


def real_basis(length, count):
    half = count // 2
    return np.concatenate(
        [
            np.cos(angle(length, np.arange(length), np.arange(half + 1))),
            np.sin(angle(length, np.arange(length), np.arange(1, half + 1))),
        ],
        axis=1,
    )


def pickers(count, padded_freqs, padded_basis):
    half = count // 2
    cos_pick = np.zeros((padded_freqs, padded_basis), np.float32)
    sin_pick = np.zeros((padded_freqs, padded_basis), np.float32)
    for place in range(count):
        freq = place - half
        cos_pick[place, abs(freq)] = 1.0
        if freq:
            sin_pick[place, half + abs(freq)] = np.sign(freq)
    return cos_pick, sin_pick


def split(x):
    high = x.astype(BF16)
    low = (x - high.astype(F32)).astype(BF16)
    return high, low


def nn(a, b):
    return lax.dot_general(a, b, (((1,), (0,)), ((), ())), preferred_element_type=F32)


def nt(a, b):
    return lax.dot_general(a, b, (((1,), (1,)), ((), ())), preferred_element_type=F32)


def tn(a, b):
    return lax.dot_general(a, b, (((0,), (0,)), ((), ())), preferred_element_type=F32)


def nn3(a, b_high, b_low):
    a_high, a_low = split(a)
    return nn(a_high, b_high) + (nn(a_high, b_low) + nn(a_low, b_high))


def exact(dot, a, b):
    return lax.dot_general(a, b, dot, precision=HIGHEST, preferred_element_type=F32)


NN = (((1,), (0,)), ((), ()))
TN = (((0,), (0,)), ((), ()))
NT = (((1,), (1,)), ((), ()))


def coeffs_kernel(mask_ref, row_ref, col_ref, out_ref, total):
    step = pl.program_id(0)

    @pl.when(step == 0)
    def _():
        total[...] = jnp.zeros_like(total)

    m_high, m_low = split(mask_ref[0])
    both = nn(row_ref[...], m_high)
    total[...] += both[:ROWS] + (both[ROWS:] + nn(row_ref[:ROWS, :], m_low))

    @pl.when(step == pl.num_programs(0) - 1)
    def _():
        r_high, r_low = split(total[...])
        res = nn(r_high, col_ref[0]) + (nn(r_high, col_ref[1]) + nn(r_low, col_ref[0]))
        for piece in range(3):
            out_ref[piece] = res[:72, piece * LANES : (piece + 1) * LANES]


def update_kernel(mask_ref, slope_ref, row_ref, col_ref, out_ref, q_ref):
    @pl.when(pl.program_id(0) == 0)
    def _():
        d = jnp.concatenate([slope_ref[0], slope_ref[1], slope_ref[2]], axis=1)
        d = jnp.concatenate([d, jnp.zeros((ROWS - 72, 3 * LANES), F32)], axis=0)
        d_high, d_low = split(d)
        q = nt(d_high, col_ref[0]) + (nt(d_high, col_ref[1]) + nt(d_low, col_ref[0]))
        q_high, q_low = split(q)
        q_ref[:ROWS] = q_high
        q_ref[ROWS : 2 * ROWS] = q_high
        q_ref[2 * ROWS :] = q_low

    out_ref[0] = mask_ref[0] - STEP_SIZE * nn(row_ref[...], q_ref[...])


def diffuse(x):
    v_len, u_len = x.shape
    up = jnp.concatenate([x[:1], x[:-1]], axis=0)
    down = jnp.concatenate([x[1:], x[-1:]], axis=0)
    left = jnp.concatenate([x[:, :1], x[:, :-1]], axis=1)
    right = jnp.concatenate([x[:, 1:], x[:, -1:]], axis=1)
    return x + DIFFUSE_RATE * (up + down + left + right - 4.0 * x)


def owner_kernel(
    ids_ref, live_ref, weight_ref, coeff_ref, target_ref, kern_ref, py_ref, px_ref, cs_ref, wy_ref,
    slope_ref, err_ref, amps, s_ref, ds_ref, intensity,
):
    slot = pl.program_id(0)
    freq_y, freq_x = kern_ref.shape[2], kern_ref.shape[3]
    kern = kern_ref.shape[1]

    def kern_pair(k):
        pad = jnp.zeros((freq_y, LANES - freq_x), F32)
        return (
            jnp.concatenate([kern_ref[0, k], pad], axis=1),
            jnp.concatenate([kern_ref[1, k], pad], axis=1),
        )

    @pl.when(live_ref[slot] == 0)
    def _():
        slope_ref[...] = jnp.zeros_like(slope_ref)

    @pl.when(slot == 0)
    def _():
        err_ref[...] = jnp.zeros_like(err_ref)

    @pl.when(live_ref[slot] != 0)
    def _():
        u = exact(NN, py_ref[...], coeff_ref[0])
        u_cos, u_sin = u[:freq_y], u[freq_y:]
        px_cos, px_sin = px_ref[0], px_ref[1]
        s_ref[0] = exact(NT, u_cos, px_cos) - exact(NT, u_sin, px_sin)
        s_ref[1] = -(exact(NT, u_sin, px_cos) + exact(NT, u_cos, px_sin))
        intensity[...] = jnp.zeros_like(intensity)

        def forward(pair, carry):
            spec_re, spec_im = s_ref[0], s_ref[1]
            rows = []
            for j in range(2):
                h_re, h_im = kern_pair(2 * pair + j)
                f_re = h_re * spec_re - h_im * spec_im
                f_im = h_re * spec_im + h_im * spec_re
                rows.append(jnp.concatenate([f_re, -f_im], axis=1))
                rows.append(jnp.concatenate([f_im, f_re], axis=1))
            f_high, f_low = split(jnp.concatenate(rows, axis=0))
            both = nt(cs_ref[...], f_high)
            x = both[:GRID_X] + (both[GRID_X:] + nt(cs_ref[:GRID_X, :], f_low))
            x_high, x_low = split(x)
            for j in range(2):
                k = 2 * pair + j
                part = slice(j * LANES, (j + 1) * LANES)
                xh, xl = x_high[:, part], x_low[:, part]
                amp = nn(jnp.concatenate([xh, xl, xh], axis=1), wy_ref[...])
                amps[k] = amp
                re, im = amp[:, :LANES], amp[:, LANES:]
                intensity[...] += weight_ref[k] * (re * re + im * im)
            return carry

        lax.fori_loop(0, kern // 2, forward, 0)
        blurred = intensity[...]
        for _ in range(DIFF_STEPS):
            blurred = diffuse(blurred)
        resist = 1.0 / (1.0 + jnp.exp(-RESIST_SLOPE * (blurred - RESIST_LEVEL)))
        offset = (GRID_X - CORE_X) // 2
        inner = resist[offset : offset + CORE_X]
        misfit = inner - target_ref[0].T
        err_ref[...] += jnp.sum(misfit * misfit, keepdims=True)
        core = (2.0 * RESIST_SLOPE) * misfit * inner * (1.0 - inner)
        edge = jnp.zeros((offset, GRID_Y), F32)
        slope = jnp.concatenate([edge, core, edge], axis=0)
        for _ in range(DIFF_STEPS):
            slope = diffuse(slope)
        intensity[...] = 2.0 * slope
        ds_ref[...] = jnp.zeros_like(ds_ref)

        def backward(k, carry):
            gain = weight_ref[k] * intensity[...]
            amp = amps[k]
            d = jnp.concatenate([gain * amp[:, :LANES], gain * amp[:, LANES:]], axis=1)
            d_high, d_low = split(d)
            w_high = wy_ref[:LANES]
            w_low = wy_ref[2 * LANES :]
            dx = nt(w_high, d_high) + (nt(w_low, d_high) + nt(w_high, d_low))
            x_high, x_low = split(dx)
            c_high, c_low = cs_ref[:GRID_X, :], cs_ref[GRID_X:, :]
            df = nn(x_high, c_high) + (nn(x_high, c_low) + nn(x_low, c_high))
            d_re, d_im = df[:freq_y], df[freq_y:]
            f_re = d_re[:, :LANES] + d_im[:, LANES:]
            f_im = d_im[:, :LANES] - d_re[:, LANES:]
            h_re, h_im = kern_pair(k)
            ds_ref[0] += h_re * f_re + h_im * f_im
            ds_ref[1] += h_re * f_im - h_im * f_re
            return carry

        lax.fori_loop(0, kern, backward, 0)
        ds_re, ds_im = ds_ref[0], ds_ref[1]
        du_cos = exact(NN, ds_re, px_cos) - exact(NN, ds_im, px_sin)
        du_sin = -(exact(NN, ds_re, px_sin) + exact(NN, ds_im, px_cos))
        slope_ref[0] = exact(TN, py_ref[...], jnp.concatenate([du_cos, du_sin], axis=0))


def tables(tile_px, freq_y, freq_x):
    win = tile_px + 2 * AMBIT
    row = np.zeros((tile_px, ROWS))
    row[:, : freq_y + 1] = real_basis(tile_px, freq_y)
    col = np.zeros((win, LANES))
    col[:, : freq_x + 1] = real_basis(win, freq_x)
    pieces = np.zeros((tile_px, 3 * LANES))
    pieces[:, :LANES] = col[AMBIT : AMBIT + tile_px]
    pieces[tile_px - AMBIT :, LANES : 2 * LANES] = col[:AMBIT]
    pieces[:AMBIT, 2 * LANES :] = col[AMBIT + tile_px :]
    r_high, r_low = halves(row)
    row_fwd = np.concatenate([r_high.T, r_low.T], axis=0)
    row_bwd = np.concatenate([r_high, r_low, r_high], axis=1)
    col_tab = np.stack(halves(pieces))
    py = np.concatenate(pickers(freq_y, freq_y, 72), axis=0)
    px = np.stack(pickers(freq_x, LANES, LANES))
    ax = angle(GRID_X, np.arange(GRID_X), np.arange(freq_x) - freq_x // 2)
    cs = np.zeros((GRID_X, 2 * LANES))
    cs[:, :freq_x] = np.cos(ax)
    cs[:, LANES : LANES + freq_x] = np.sin(ax)
    cs = np.concatenate(halves(cs), axis=0)
    ay = angle(GRID_Y, np.arange(freq_y) - freq_y // 2, np.arange(GRID_Y))
    wy = np.block([[np.cos(ay), np.sin(ay)], [-np.sin(ay), np.cos(ay)]]) / (64.0 * GRID_Y * GRID_X)
    w_high, w_low = halves(wy)
    wy = np.concatenate([w_high, w_high, w_low], axis=0)
    return row_fwd, row_bwd, col_tab, py, px, cs, wy


def whole(shape, memory_space=None):
    return pl.BlockSpec(shape, lambda *_: (0,) * len(shape))


def on_device(mask_tiles, target_grid, kernels, kern_weight, owner_list):
    tile_px = mask_tiles.shape[1]
    kern, freq_y, freq_x = kernels.shape[2:]
    count = lax.axis_size("tile")
    row_fwd, row_bwd, col_tab, py, px, cs, wy = tables(tile_px, freq_y, freq_x)
    me = lax.axis_index("tile")

    mine = owner_list[:, 0] == me
    places = jnp.arange(count, dtype=jnp.int32)
    first = jnp.min(jnp.where(mine, places, count))
    last = jnp.max(jnp.where(mine, places, -1))
    ids = jnp.stack([jnp.minimum(first, count - 1), jnp.maximum(last, 0)])
    live = jnp.stack([first < count, last > first]).astype(jnp.int32)

    targets = lax.all_gather(target_grid.reshape(GRID_Y, CORE_X), "tile", axis=0)

    chunk = 256
    steps = tile_px // chunk
    pieces = pl.pallas_call(
        coeffs_kernel,
        grid=(steps,),
        in_specs=[
            pl.BlockSpec((1, chunk, tile_px), lambda i: (0, i, 0)),
            pl.BlockSpec((2 * ROWS, chunk), lambda i: (0, i)),
            whole(col_tab.shape),
        ],
        out_specs=whole((3, 72, LANES)),
        out_shape=jax.ShapeDtypeStruct((3, 72, LANES), F32),
        scratch_shapes=[pltpu.VMEM((ROWS, tile_px), F32)],
        compiler_params=pltpu.CompilerParams(vmem_limit_bytes=40 << 20),
        name="coeffs",
    )(mask_tiles, row_fwd, col_tab)

    ring = [(i, i + 1) for i in range(count - 1)]
    from_left = lax.ppermute(pieces[1], "tile", ring)
    from_right = lax.ppermute(pieces[2], "tile", [(b, a) for a, b in ring])
    coeffs = lax.all_gather(pieces[0] + from_left + from_right, "tile", axis=0)

    slopes, errors = pl.pallas_call(
        owner_kernel,
        grid_spec=pltpu.PrefetchScalarGridSpec(
            num_scalar_prefetch=3,
            grid=(MOST,),
            in_specs=[
                pl.BlockSpec((1, 72, LANES), lambda s, ids, live, w: (ids[s], 0, 0)),
                pl.BlockSpec((1, GRID_Y, CORE_X), lambda s, ids, live, w: (ids[s], 0, 0)),
                whole((2, kern, freq_y, freq_x)),
                whole(py.shape),
                whole(px.shape),
                whole(cs.shape),
                whole(wy.shape),
            ],
            out_specs=[
                pl.BlockSpec((1, 72, LANES), lambda s, *_: (s, 0, 0)),
                whole((1, 1)),
            ],
            scratch_shapes=[
                pltpu.VMEM((kern, GRID_X, 2 * GRID_Y), F32),
                pltpu.VMEM((2, freq_y, LANES), F32),
                pltpu.VMEM((2, freq_y, LANES), F32),
                pltpu.VMEM((GRID_X, GRID_Y), F32),
            ],
        ),
        out_shape=[
            jax.ShapeDtypeStruct((MOST, 72, LANES), F32),
            jax.ShapeDtypeStruct((1, 1), F32),
        ],
        compiler_params=pltpu.CompilerParams(vmem_limit_bytes=40 << 20),
        name="owner",
    )(ids, live, kern_weight, coeffs, targets, kernels[0], py, px, cs, wy)

    gathered = lax.all_gather(slopes, "tile", axis=0)
    owners = owner_list[:, 0]
    same = owners[:, None] == owners[None, :]
    rank = jnp.sum(same & (places[None, :] < places[:, None]), axis=1).astype(jnp.int32)

    def slope_of(tile):
        inside = jnp.clip(tile, 0, count - 1)
        flat = gathered.reshape(count * MOST, 72, LANES)
        place = owners[inside] * MOST + rank[inside]
        found = lax.dynamic_index_in_dim(flat, place, 0, keepdims=False)
        return jnp.where(inside == tile, found, 0.0)

    my_slopes = jnp.stack([slope_of(me), slope_of(me + 1), slope_of(me - 1)])
    out = pl.pallas_call(
        update_kernel,
        grid=(steps,),
        in_specs=[
            pl.BlockSpec((1, chunk, tile_px), lambda i: (0, i, 0)),
            whole((3, 72, LANES)),
            pl.BlockSpec((chunk, 3 * ROWS), lambda i: (i, 0)),
            whole(col_tab.shape),
        ],
        out_specs=pl.BlockSpec((1, chunk, tile_px), lambda i: (0, i, 0)),
        out_shape=jax.ShapeDtypeStruct(mask_tiles.shape, F32),
        scratch_shapes=[pltpu.VMEM((3 * ROWS, tile_px), BF16)],
        compiler_params=pltpu.CompilerParams(vmem_limit_bytes=40 << 20),
        name="update",
    )(mask_tiles, my_slopes, row_bwd, col_tab)
    return out, (errors / (GRID_Y * CORE_X)).reshape(1)


def solution(mesh):
    placed = (
        P(("stripe", "tile"), None, None),
        P(("stripe", "tile"), None),
        P("tile", None, None, None, None),
        P(),
        P("stripe", None),
    )
    return jax.shard_map(
        on_device,
        mesh=mesh,
        in_specs=placed,
        out_specs=(P(("stripe", "tile"), None, None), P(("stripe", "tile"))),
        check_vma=False,
    )
```

profile of v0, /device:TPU:0, one launch (start us, length us, event | category | flops | bytes accessed | tf_op | source)
XLA Modules:
  0.0 151.3 jit_solution(4063243764415225560)
XLA Ops:
  7.2 0.0 all-gather.5.cloned.1.call-start
  7.2 0.7 all-gather.5.cloned.1.call-update
  7.9 0.0 all-gather.7.cloned.1.call-start
  7.9 0.0 copy-start
  8.0 2.2 %copy-done = f32[1,1024,1024]{2,1,0:T(8,128)S(1)} copy-done((f32[1,1024,1024]{2,1,0:T(8,128)S(1)}, f32[1,1024,1024]{2,1,0:T(8,128)}, u32[]{:S(2)}) %copy-start) | copy-done | bytes 4194328
  10.1 0.0 copy-start.2
  10.1 1.4 copy-done.2
  11.5 0.0 copy-start.7
  11.5 1.0 copy-done.7
  12.5 0.0 copy-start.13
  12.5 0.0 copy-start.8
  12.5 0.0 copy-start.10
  12.5 0.0 copy-start.11
  12.5 0.0 copy-start.12
  12.6 2.0 %coeffs.1 = f32[3,72,128]{2,1,0:T(8,128)S(1)} custom-call(f32[1,1024,1024]{2,1,0:T(8,128)S(1)} %copy-done, bf16[160,1024]{1,0:T(8,128)(2,1)S(1)} %copy-done.7, bf16[2,1024,384]{2,1,0:T(8,128)(2,1)S(1)} %copy-done.2), custom_call_target="tpu_custom_call" | custom-call | tf_op jit(solution)/shard_map/coeffs/pallas_call | solution.py:288
  14.6 2.4 %collective-permute-start = (f32[72,128]{1,0:T(8,128)S(1)}, f32[72,128]{1,0:T(8,128)S(1)}, u32[]{:S(2)}, u32[]{:S(2)}) collective-permute-start(f32[72,128]{1,0:T(8,128)S(1)} %get-tuple-element.11), channel_id=1, source_target_pairs={{0,1},{1,2},{2,3},{3,4},{4,5},{5,6},{6,7},{7,8},{8,9},{9,10},{10,1... | collective-permute-start | bytes 110600 | tf_op jit(solution)/shard_map/ppermute | solution.py:304
  17.0 1.3 collective-permute-start.1
  18.3 0.0 copy-done.13
  18.3 0.6 fusion.3
  22.2 0.1 pad_add_fusion.ids_ref
  22.2 0.1 add_convert_fusion.live_ref
  22.3 0.0 collective-permute-done
  22.3 0.0 collective-permute-done.1
  22.3 27.2 %all-gather = f32[1152,128]{1,0:T(8,128)S(1)} all-gather(f32[72,128]{1,0:T(8,128)S(1)} %fusion.1), channel_id=2, replica_groups=mesh['stripe'=2,'tile'=16] {'tile'}, dimensions={0}, use_global_device_ids=true | all-gather | bytes 626688 | tf_op jit(solution)/shard_map/all_gather | solution.py:306
  49.5 2.4 %all-gather.5.cloned.1.call-done.target_ref = f32[16,128,128]{2,1,0:T(8,128)} async-done(((f32[1,128,128]{2,1,0:T(8,128)}), f32[16,128,128]{2,1,0:T(8,128)}) %all-gather.5.cloned.1.call-update) | async-done | bytes 1048592 | tf_op jit(solution)/shard_map/all_gather | solution.py:284
  52.0 0.0 copy-done.8
  52.0 0.0 copy-done.9
  52.0 0.0 copy-done.10
  52.0 0.0 copy-done.11
  52.0 0.0 copy-done.12
  52.0 0.0 copy-start.4
  52.0 1.4 copy-done.4
  53.4 0.0 copy-start.5
  53.4 1.2 copy-done.5
  54.6 0.0 copy-start.3
  54.6 0.0 copy-start.6
  54.6 1.2 owner.1
  55.9 0.0 all-gather.7.cloned.1.call-update
  55.9 0.7 constant_dynamic-slice_fusion.2
  57.1 0.2 convert_reduce_fusion
  57.3 0.7 fusion.5
  61.7 74.9 %all-gather.7.cloned.1.call-done = f32[32,72,128]{2,1,0:T(8,128)} async-done(((f32[2,72,128]{2,1,0:T(8,128)}), f32[32,72,128]{2,1,0:T(8,128)}) %all-gather.7.cloned.1.call-update) | async-done | bytes 1179664 | tf_op jit(solution)/shard_map/all_gather | solution.py:341
  136.5 0.9 dynamic-slice_select_fusion
  137.4 0.0 copy-done.3
  137.4 0.0 copy-done.6
  137.4 0.0 copy-start.1
  137.4 2.2 %copy-done.1 = f32[1,1024,1024]{2,1,0:T(8,128)S(1)} copy-done((f32[1,1024,1024]{2,1,0:T(8,128)S(1)}, f32[1,1024,1024]{2,1,0:T(8,128)}, u32[]{:S(2)}) %copy-start.1) | copy-done | bytes 4194328
  139.6 3.7 %update.1 = f32[1,1024,1024]{2,1,0:T(8,128)} custom-call(f32[1,1024,1024]{2,1,0:T(8,128)S(1)} %copy-done.1, f32[3,72,128]{2,1,0:T(8,128)S(1)} %pad_maximum_fusion.slope_ref, bf16[1024,240]{1,0:T(8,128)(2,1)S(1)} %copy-done.6, bf16[2,1024,384]{2,1,0:T(8,128)(2,1)S(1)} %copy-done.3), custom_call_target="tpu_custom_call" | custom-call | tf_op jit(solution)/shard_map/update/pallas_call | solution.py:354
  (4 shorter events, 0.0 us)
Async XLA Ops:
  7.2 44.8 %all-gather.5.cloned.1.call-start = ((), (), s32[]{:S(2)}) async-start(), calls=%async_computation | async-start | bytes 1114112 | tf_op jit(solution)/shard_map/all_gather | solution.py:284
  7.9 128.6 %all-gather.7.cloned.1.call-start = ((), (), s32[]{:S(2)}) async-start(), calls=%async_computation.1 | async-start | bytes 1253376 | tf_op jit(solution)/shard_map/all_gather | solution.py:341
  7.9 2.2 %copy-start = (f32[1,1024,1024]{2,1,0:T(8,128)S(1)}, f32[1,1024,1024]{2,1,0:T(8,128)}, u32[]{:S(2)}) copy-start(f32[1,1024,1024]{2,1,0:T(8,128)} %mask_ref.3) | copy-start | bytes 12582916
  10.1 1.4 copy-start.2
  11.5 1.0 copy-start.7
  12.5 5.7 %copy-start.13 = (s32[16,1]{0,1:T(1,128)S(1)}, s32[16,1]{0,1:T(1,128)}, u32[]{:S(2)}) copy-start(s32[16,1]{0,1:T(1,128)} %param.16) | copy-start | bytes 196
  12.5 39.4 %copy-start.8 = (bf16[384,256]{1,0:T(8,128)(2,1)S(1)}, bf16[384,256]{1,0:T(8,128)(2,1)}, u32[]{:S(2)}) copy-start(bf16[384,256]{1,0:T(8,128)(2,1)} %constant.63.clone.wy_ref) | copy-start | bytes 589828
  12.5 39.4 %copy-start.9 = (bf16[384,256]{1,0:T(8,128)(2,1)S(1)}, bf16[384,256]{1,0:T(8,128)(2,1)}, u32[]{:S(2)}) copy-start(bf16[384,256]{1,0:T(8,128)(2,1)} %constant.62.clone.cs_ref) | copy-start | bytes 589828
  12.5 39.4 %copy-start.10 = (f32[2,128,128]{2,1,0:T(8,128)S(1)}, f32[2,128,128]{2,1,0:T(8,128)}, u32[]{:S(2)}) copy-start(f32[2,128,128]{2,1,0:T(8,128)} %constant.61.clone.px_ref) | copy-start | bytes 393220
  12.5 39.4 %copy-start.11 = (f32[128,72]{1,0:T(8,128)S(1)}, f32[128,72]{1,0:T(8,128)}, u32[]{:S(2)}) copy-start(f32[128,72]{1,0:T(8,128)} %constant.60.clone.py_ref) | copy-start | bytes 110596
  12.5 39.4 %copy-start.12 = (f32[24]{0:T(128)S(1)}, f32[24]{0:T(128)}, u32[]{:S(2)}) copy-start(f32[24]{0:T(128)} %weight_ref.1) | copy-start | bytes 292
  14.6 7.7 %collective-permute-start = (f32[72,128]{1,0:T(8,128)S(1)}, f32[72,128]{1,0:T(8,128)S(1)}, u32[]{:S(2)}, u32[]{:S(2)}) collective-permute-start(f32[72,128]{1,0:T(8,128)S(1)} %get-tuple-element.11), channel_id=1, source_target_pairs={{0,1},{1,2},{2,3},{3,4},{4,5},{5,6},{6,7},{7,8},{8,9},{9,10},{10,1... | collective-permute-start | bytes 110600 | tf_op jit(solution)/shard_map/ppermute | solution.py:304
  17.0 5.4 %collective-permute-start.1 = (f32[72,128]{1,0:T(8,128)S(1)}, f32[72,128]{1,0:T(8,128)S(1)}, u32[]{:S(2)}, u32[]{:S(2)}) collective-permute-start(f32[72,128]{1,0:T(8,128)S(1)} %get-tuple-element.12), channel_id=1, source_target_pairs={{1,0},{2,1},{3,2},{4,3},{5,4},{6,5},{7,6},{8,7},{9,8},{10,9},{11,1... | collective-permute-start | bytes 110600 | tf_op jit(solution)/shard_map/ppermute | solution.py:305
  52.0 1.4 copy-start.4
  53.4 1.2 copy-start.5
  54.6 82.8 %copy-start.3 = (bf16[2,1024,384]{2,1,0:T(8,128)(2,1)S(1)}, bf16[2,1024,384]{2,1,0:T(8,128)(2,1)}, u32[]{:S(2)}) copy-start(bf16[2,1024,384]{2,1,0:T(8,128)(2,1)} %constant.59.clone.col_ref) | copy-start | bytes 4718596
  54.6 82.8 %copy-start.6 = (bf16[1024,240]{1,0:T(8,128)(2,1)S(1)}, bf16[1024,240]{1,0:T(8,128)(2,1)}, u32[]{:S(2)}) copy-start(bf16[1024,240]{1,0:T(8,128)(2,1)} %constant.64.clone.row_ref) | copy-start | bytes 1474564
  137.4 2.2 %copy-start.1 = (f32[1,1024,1024]{2,1,0:T(8,128)S(1)}, f32[1,1024,1024]{2,1,0:T(8,128)}, u32[]{:S(2)}) copy-start(f32[1,1024,1024]{2,1,0:T(8,128)} %mask_ref.3) | copy-start | bytes 12582916
Sparse Core Ops, SparseCore 0:
  10.2 41.7 all-gather.4
  56.0 80.4 all-gather.6
where the time goes:
time: 152 us; the launch traced here: 151 us
  waiting for transfers between devices  78 us (51%)
  blocking collectives  27.2 us (18%)
  between operations  22.8 us (15%)
  local copies, waits for them, and re-layouts  10.7 us (7%)
  Pallas kernels  6.98 us (5%)
  starting transfers between devices  3.73 us (2%)
  other arithmetic  1.84 us (1%)
    all_gather x1, waiting for transfers between devices, on_device(): gathered = lax.all_gather(slopes, 'tile', axis=0)  74.9 us
    all_gather x1, blocking collectives, on_device(): coeffs = lax.all_gather(pieces[0] + from_left + from_right, 'tile', axis=0)  27.2 us
    unnamed x28, local copies, waits for them, and re-layouts  9.41 us
    pallas_call x1, Pallas kernels, on_device(): pl.pallas_call(update_kernel, grid=(steps,), in_specs=[pl.BlockSpec((1, c...  3.72 us
  transfers between devices with their start and end apart: 4, of which 2 were waited for; matrix products, arithmetic and copies ran while one was open for 2% of the time, Pallas kernels for 1%

commit v1 on v0

--- a/solution.py
+++ b/solution.py
@@ -17,6 +17,7 @@
 MOST = 2
 ROWS = 80
 LANES = 128
+VMEM_BYTES = 60 << 20
 
 RESIST_SLOPE = 3.0
 RESIST_LEVEL = 1.2
@@ -233,6 +234,161 @@
         du_cos = exact(NN, ds_re, px_cos) - exact(NN, ds_im, px_sin)
         du_sin = -(exact(NN, ds_re, px_sin) + exact(NN, ds_im, px_cos))
         slope_ref[0] = exact(TN, py_ref[...], jnp.concatenate([du_cos, du_sin], axis=0))
+
+
+def factors(count):
+    pair = 2 if count % 2 == 0 else 1
+    rest = count // pair
+    inner = max(d for d in range(1, rest + 1) if rest % d == 0 and d * d <= rest)
+    return rest // inner, inner, pair
+
+
+def wrapped(index, size):
+    return lax.rem(index + size, size)
+
+
+class Place:
+    def __init__(self, count):
+        self.count = count
+        self.outer, self.inner, self.pair = factors(count)
+        self.me = lax.axis_index("tile")
+        self.c = lax.rem(self.me, self.pair)
+        self.b = lax.rem(self.me // self.pair, self.inner)
+        self.a = self.me // (self.pair * self.inner)
+
+    def at(self, da, db, dc):
+        a = wrapped(self.a + da, self.outer)
+        b = wrapped(self.b + db, self.inner)
+        c = wrapped(self.c + dc, self.pair)
+        return (a * self.inner + b) * self.pair + c
+
+    def partners(self):
+        return (
+            [self.at(d, 0, 0) for d in range(1, self.outer)]
+            + [self.at(0, d, 0) for d in range(1, self.inner)]
+            + [self.at(0, 0, d) for d in range(1, self.pair)]
+        )
+
+
+def meet(devices):
+    barrier = pltpu.get_barrier_semaphore()
+    for device in devices:
+        pl.semaphore_signal(
+            barrier, inc=1, device_id={"tile": device}, device_id_type=pl.DeviceIdType.MESH
+        )
+    pl.semaphore_wait(barrier, len(devices))
+
+
+class Gather:
+    def __init__(self, place, slots, send, recv):
+        self.place, self.slots, self.send, self.recv = place, slots, send, recv
+        self.started = []
+
+    def copy(self, slot, device, index):
+        return pltpu.make_async_remote_copy(
+            src_ref=self.slots.at[slot],
+            dst_ref=self.slots.at[slot],
+            send_sem=self.send.at[index],
+            recv_sem=self.recv.at[slot],
+            device_id={"tile": device},
+            device_id_type=pl.DeviceIdType.MESH,
+        )
+
+    def push(self, slot, device):
+        copy = self.copy(slot, device, len(self.started))
+        copy.start()
+        self.started.append(copy)
+
+    def arrive(self, slot):
+        self.copy(slot, self.place.at(1, 0, 0), 0).wait_recv()
+
+    def to_pair(self, slot):
+        for d in range(1, self.place.pair):
+            self.push(slot, self.place.at(0, 0, d))
+
+    def to_inner(self, slot):
+        for d in range(1, self.place.inner):
+            self.push(slot, self.place.at(0, d, 0))
+
+    def own(self):
+        p = self.place
+        for d in range(1, p.outer):
+            self.push(p.me, p.at(d, 0, 0))
+        self.to_inner(p.me)
+        self.to_pair(p.me)
+
+    def outer_arrivals(self):
+        for d in range(1, self.place.outer):
+            slot = self.place.at(-d, 0, 0)
+            self.arrive(slot)
+            self.to_inner(slot)
+            self.to_pair(slot)
+
+    def inner_arrivals(self):
+        for d in range(self.place.outer):
+            for e in range(1, self.place.inner):
+                slot = self.place.at(-d, -e, 0)
+                self.arrive(slot)
+                self.to_pair(slot)
+
+    def finish(self):
+        p = self.place
+        for d in range(p.outer):
+            for e in range(p.inner):
+                for f in range(1, p.pair):
+                    self.arrive(p.at(-d, -e, -f))
+        for copy in self.started:
+            copy.wait_send()
+
+
+def spread_kernel(
+    count, piece_ref, target_ref, coeff_ref, all_target_ref, near, near_send, near_recv,
+    send_c, recv_c, send_t, recv_t,
+):
+    place = Place(count)
+    me = place.me
+    right, left = wrapped(me + 1, count), wrapped(me - 1, count)
+    coeff = Gather(place, coeff_ref, send_c, recv_c)
+    target = Gather(place, all_target_ref, send_t, recv_t)
+    all_target_ref[me] = target_ref[...]
+    meet([right, left] + place.partners())
+    sides = []
+    for side, device in ((0, right), (1, left)):
+        copy = pltpu.make_async_remote_copy(
+            src_ref=piece_ref.at[1 + side],
+            dst_ref=near.at[side],
+            send_sem=near_send.at[side],
+            recv_sem=near_recv.at[side],
+            device_id={"tile": device},
+            device_id_type=pl.DeviceIdType.MESH,
+        )
+        copy.start()
+        sides.append(copy)
+    target.own()
+    for copy in sides:
+        copy.wait()
+    own = piece_ref[0]
+    own = own + jnp.where(me > 0, near[0], 0.0)
+    own = own + jnp.where(me < count - 1, near[1], 0.0)
+    coeff_ref[me] = own
+    coeff.own()
+    target.outer_arrivals()
+    coeff.outer_arrivals()
+    target.inner_arrivals()
+    coeff.inner_arrivals()
+    target.finish()
+    coeff.finish()
+
+
+def collect_kernel(count, slope_ref, all_ref, send, recv):
+    place = Place(count)
+    gather = Gather(place, all_ref, send, recv)
+    all_ref[place.me] = slope_ref[...]
+    meet(place.partners())
+    gather.own()
+    gather.outer_arrivals()
+    gather.inner_arrivals()
+    gather.finish()
 
 
 def tables(tile_px, freq_y, freq_x):
@@ -281,8 +437,6 @@
     ids = jnp.stack([jnp.minimum(first, count - 1), jnp.maximum(last, 0)])
     live = jnp.stack([first < count, last > first]).astype(jnp.int32)
 
-    targets = lax.all_gather(target_grid.reshape(GRID_Y, CORE_X), "tile", axis=0)
-
     chunk = 256
     steps = tile_px // chunk
     pieces = pl.pallas_call(
@@ -296,14 +450,27 @@
         out_specs=whole((3, 72, LANES)),
         out_shape=jax.ShapeDtypeStruct((3, 72, LANES), F32),
         scratch_shapes=[pltpu.VMEM((ROWS, tile_px), F32)],
-        compiler_params=pltpu.CompilerParams(vmem_limit_bytes=40 << 20),
+        compiler_params=pltpu.CompilerParams(vmem_limit_bytes=VMEM_BYTES),
         name="coeffs",
     )(mask_tiles, row_fwd, col_tab)
 
-    ring = [(i, i + 1) for i in range(count - 1)]
-    from_left = lax.ppermute(pieces[1], "tile", ring)
-    from_right = lax.ppermute(pieces[2], "tile", [(b, a) for a, b in ring])
-    coeffs = lax.all_gather(pieces[0] + from_left + from_right, "tile", axis=0)
+    vmem = pl.BlockSpec(memory_space=pltpu.VMEM)
+    dma = pltpu.SemaphoreType.DMA
+    coeffs, targets = pl.pallas_call(
+        functools.partial(spread_kernel, count),
+        in_specs=[vmem, vmem],
+        out_specs=[vmem, vmem],
+        out_shape=[
+            jax.ShapeDtypeStruct((count, 72, LANES), F32),
+            jax.ShapeDtypeStruct((count, GRID_Y, CORE_X), F32),
+        ],
+        scratch_shapes=[pltpu.VMEM((2, 72, LANES), F32), dma((2,)), dma((2,))]
+        + [dma((count,))] * 4,
+        compiler_params=pltpu.CompilerParams(
+            collective_id=0, has_side_effects=True, vmem_limit_bytes=VMEM_BYTES
+        ),
+        name="spread",
+    )(pieces, target_grid.reshape(GRID_Y, CORE_X))
 
     slopes, errors = pl.pallas_call(
         owner_kernel,
@@ -334,11 +501,21 @@
             jax.ShapeDtypeStruct((MOST, 72, LANES), F32),
             jax.ShapeDtypeStruct((1, 1), F32),
         ],
-        compiler_params=pltpu.CompilerParams(vmem_limit_bytes=40 << 20),
+        compiler_params=pltpu.CompilerParams(vmem_limit_bytes=VMEM_BYTES),
         name="owner",
     )(ids, live, kern_weight, coeffs, targets, kernels[0], py, px, cs, wy)
 
-    gathered = lax.all_gather(slopes, "tile", axis=0)
+    gathered = pl.pallas_call(
+        functools.partial(collect_kernel, count),
+        in_specs=[vmem],
+        out_specs=vmem,
+        out_shape=jax.ShapeDtypeStruct((count, MOST, 72, LANES), F32),
+        scratch_shapes=[dma((count,))] * 2,
+        compiler_params=pltpu.CompilerParams(
+            collective_id=1, has_side_effects=True, vmem_limit_bytes=VMEM_BYTES
+        ),
+        name="collect",
+    )(slopes)
     owners = owner_list[:, 0]
     same = owners[:, None] == owners[None, :]
     rank = jnp.sum(same & (places[None, :] < places[:, None]), axis=1).astype(jnp.int32)
@@ -363,7 +540,7 @@
         out_specs=pl.BlockSpec((1, chunk, tile_px), lambda i: (0, i, 0)),
         out_shape=jax.ShapeDtypeStruct(mask_tiles.shape, F32),
         scratch_shapes=[pltpu.VMEM((3 * ROWS, tile_px), BF16)],
-        compiler_params=pltpu.CompilerParams(vmem_limit_bytes=40 << 20),
+        compiler_params=pltpu.CompilerParams(vmem_limit_bytes=VMEM_BYTES),
         name="update",
     )(mask_tiles, my_slopes, row_bwd, col_tab)
     return out, (errors / (GRID_Y * CORE_X)).reshape(1)

time: 152 us -> 114 us (0.75)
  Pallas kernels: 6.98 us -> 97 us
  waiting for transfers between devices: 78 us -> 0 us
  blocking collectives: 27.2 us -> 0 us
  between operations: 22.8 us -> 9.52 us
  local copies, waits for them, and re-layouts: 10.7 us -> 2.08 us
  starting transfers between devices: 3.73 us -> 0 us
  other arithmetic: 1.84 us -> 4.86 us
    pallas_call x0 -> x2, Pallas kernels: none -> 82 us  [the longest x1 59.6 us: on_device(): pl.pallas_call(functools.partial(collect_kernel, count), in_specs=[vmem],...]
    all_gather x2 -> x0, waiting for transfers between devices: 77.3 us -> none  [the longest x1 74.9 us: on_device(): gathered = lax.all_gather(slopes, 'tile', axis=0)]
    all_gather x1 -> x0, blocking collectives: 27.2 us -> none  [on_device(): coeffs = lax.all_gather(pieces[0] + from_left + from_right, 'tile', axis=0)]
    unnamed x28 -> x0, local copies, waits for them, and re-layouts: 9.41 us -> none
    ppermute x2 -> x0, starting transfers between devices: 3.66 us -> none  [the longest x1 2.37 us: on_device(): from_left = lax.ppermute(pieces[1], 'tile', ring)]
    pallas_call x1, Pallas kernels: 2.01 us -> 5.32 us  [on_device(): pl.pallas_call(coeffs_kernel, grid=(steps,), in_specs=[pl.BlockSpec((1, c...]
    pallas_call x1, Pallas kernels: 3.72 us -> 6.64 us  [on_device(): pl.pallas_call(update_kernel, grid=(steps,), in_specs=[pl.BlockSpec((1, c...]
    pallas_call x1, Pallas kernels: 1.25 us -> 2.99 us  [on_device(): pl.pallas_call(owner_kernel, grid_spec=pltpu.PrefetchScalarGridSpec(num_s...]
  transfers between devices with their start and end apart: 4 -> 0, of which waited for: 2 -> 0; matrix products, arithmetic and copies ran while one was open for 2% -> 0% of each run, Pallas kernels for 1% -> 0%
where the time goes in v1:
time: 114 us; the launch traced here: 113 us
  Pallas kernels  97 us (85%)
  between operations  9.52 us (8%)
  other arithmetic  4.86 us (4%)
  local copies, waits for them, and re-layouts  2.08 us (2%)
    pallas_call x1, Pallas kernels, on_device(): pl.pallas_call(functools.partial(collect_kernel, count), in_specs=[vmem],...  59.6 us
    pallas_call x1, Pallas kernels, on_device(): pl.pallas_call(functools.partial(spread_kernel, count), in_specs=[vmem, v...  22.5 us
    pallas_call x1, Pallas kernels, on_device(): pl.pallas_call(update_kernel, grid=(steps,), in_specs=[pl.BlockSpec((1, c...  6.64 us
    pallas_call x1, Pallas kernels, on_device(): pl.pallas_call(coeffs_kernel, grid=(steps,), in_specs=[pl.BlockSpec((1, c...  5.32 us
    pallas_call x1, Pallas kernels, on_device(): pl.pallas_call(owner_kernel, grid_spec=pltpu.PrefetchScalarGridSpec(num_s...  2.99 us

profile of v1, /device:TPU:0, one launch (start us, length us, event | category | flops | bytes accessed | tf_op | source)
XLA Modules:
  0.0 113.4 jit_solution(618820680452138425)
XLA Ops:
  0.6 0.9 convert_reduce_fusion
  1.6 1.3 %fusion.1 = (s32[]{:T(128)}, s32[]{:T(128)}) fusion(s32[]{:T(128)S(6)} %axis_index.12, s32[16,1]{0,1:T(1,128)} %param.16), kind=kLoop, calls=%fused_computation.13 | loop fusion | flops 78 | bytes 76 | tf_op jit(solution)/shard_map/reduce_min | solution.py:435
  6.1 0.6 pad_add_fusion.ids_ref
  6.7 0.6 add_convert_fusion.live_ref
  7.2 0.7 fusion.3
  7.9 1.4 %constant_dynamic-slice_fusion.2 = (s32[1,1]{0,1:T(1,128)}, s32[1,1]{0,1:T(1,128)}, s32[1,1]{0,1:T(1,128)}) fusion(s32[16,1]{0,1:T(1,128)} %param.16, s32[]{:T(128)S(6)} %min.13, s32[]{:T(128)S(6)} %min.16, s32[]{:T(128)S(6)} %min.15), kind=kLoop, calls=%fused_computation.10 | loop fusion | bytes 36 | tf_op jit(solution)/shard_map/dynamic_slice | solution.py:526
  13.1 5.3 %coeffs.1.piece_ref = f32[3,72,128]{2,1,0:T(8,128)} custom-call(f32[1,1024,1024]{2,1,0:T(8,128)} %mask_ref.3, bf16[160,1024]{1,0:T(8,128)(2,1)} %constant.58.clone.row_ref, bf16[2,1024,384]{2,1,0:T(8,128)(2,1)} %constant.59.clone.col_ref), custom_call_target="tpu_custom_call" | custom-call | tf_op jit(solution)/shard_map/coeffs/pallas_call | solution.py:442
  18.4 22.5 %spread.1 = (f32[16,72,128]{2,1,0:T(8,128)}, f32[16,128,128]{2,1,0:T(8,128)}) custom-call(f32[3,72,128]{2,1,0:T(8,128)} %coeffs.1.piece_ref, f32[128,128]{1,0:T(8,128)} %bitcast.19), custom_call_target="tpu_custom_call" | custom-call | tf_op jit(solution)/shard_map/spread/pallas_call | solution.py:459
  40.9 3.0 %owner.1 = (f32[2,72,128]{2,1,0:T(8,128)}, f32[1,1]{1,0:T(1,128)}) custom-call(s32[2]{0:T(128)} %pad_add_fusion.ids_ref, s32[2]{0:T(128)} %add_convert_fusion.live_ref, f32[24]{0:T(128)} %weight_ref.1, f32[16,72,128]{2,1,0:T(8,128)} %get-tuple-element.6.coeff_ref, f32[16,128,128]{2,1,0:T(8,128)} %get-tuple-element.7.target_ref, f32[2,24,64,96]{3,2,1,0:T(8,128)} %bitcast.17, ...), custom_call_target="tpu_custom_call" | custom-call | tf_op jit(solution)/shard_map/owner/pallas_call | solution.py:475
  44.6 59.6 %collect.1 = f32[16,2,72,128]{3,2,1,0:T(8,128)} custom-call(f32[2,72,128]{2,1,0:T(8,128)} %get-tuple-element.8.slope_ref), custom_call_target="tpu_custom_call" | custom-call | tf_op jit(solution)/shard_map/collect/pallas_call | solution.py:508
  104.1 0.9 dynamic-slice_select_fusion.2
  105.0 0.6 pad_maximum_fusion.slope_ref
  105.7 6.6 %update.1 = f32[1,1024,1024]{2,1,0:T(8,128)} custom-call(f32[1,1024,1024]{2,1,0:T(8,128)} %mask_ref.3, f32[3,72,128]{2,1,0:T(8,128)} %pad_maximum_fusion.slope_ref, bf16[1024,240]{1,0:T(8,128)(2,1)} %constant.64.clone.row_ref, bf16[2,1024,384]{2,1,0:T(8,128)(2,1)} %constant.59.clone.col_ref), custom_call_target="tpu_custom_call" | custom-call | tf_op jit(solution)/shard_map/update/pallas_call | solution.py:531

commit v2 on v1

--- a/solution.py
+++ b/solution.py
@@ -114,10 +114,21 @@
             out_ref[piece] = res[:72, piece * LANES : (piece + 1) * LANES]
 
 
-def update_kernel(mask_ref, slope_ref, row_ref, col_ref, out_ref, q_ref):
+def update_kernel(mask_ref, owners_ref, slope_ref, row_ref, col_ref, out_ref, q_ref):
     @pl.when(pl.program_id(0) == 0)
     def _():
-        d = jnp.concatenate([slope_ref[0], slope_ref[1], slope_ref[2]], axis=1)
+        count = slope_ref.shape[0]
+        me = lax.axis_index("tile")
+
+        def slope_of(tile):
+            inside = jnp.clip(tile, 0, count - 1)
+            owner = owners_ref[inside]
+            rank = lax.fori_loop(
+                0, inside, lambda i, r: jnp.where(owners_ref[i] == owner, 1, r), jnp.int32(0)
+            )
+            return jnp.where(inside == tile, slope_ref[owner, rank], 0.0)
+
+        d = jnp.concatenate([slope_of(me), slope_of(me + 1), slope_of(me - 1)], axis=1)
         d = jnp.concatenate([d, jnp.zeros((ROWS - 72, 3 * LANES), F32)], axis=0)
         d_high, d_low = split(d)
         q = nt(d_high, col_ref[0]) + (nt(d_high, col_ref[1]) + nt(d_low, col_ref[0]))
@@ -139,12 +150,24 @@
 
 
 def owner_kernel(
-    ids_ref, live_ref, weight_ref, coeff_ref, target_ref, kern_ref, py_ref, px_ref, cs_ref, wy_ref,
-    slope_ref, err_ref, amps, s_ref, ds_ref, intensity,
+    owners_ref, weight_ref, coeffs_ref, targets_ref, kern_ref, py_ref, px_ref, cs_ref, wy_ref,
+    slope_ref, err_ref, amps, errors,
 ):
-    slot = pl.program_id(0)
     freq_y, freq_x = kern_ref.shape[2], kern_ref.shape[3]
     kern = kern_ref.shape[1]
+    count = coeffs_ref.shape[0]
+    me = lax.axis_index("tile")
+
+    def look(place, found):
+        first, last = found
+        mine = owners_ref[place] == me
+        return (
+            jnp.where(mine & (first == count), place, first),
+            jnp.where(mine, place, last),
+        )
+
+    first, last = lax.fori_loop(0, count, look, (jnp.int32(count), jnp.int32(-1)))
+    errors[...] = jnp.zeros_like(errors)
 
     def kern_pair(k):
         pad = jnp.zeros((freq_y, LANES - freq_x), F32)
@@ -153,25 +176,28 @@
             jnp.concatenate([kern_ref[1, k], pad], axis=1),
         )
 
-    @pl.when(live_ref[slot] == 0)
-    def _():
-        slope_ref[...] = jnp.zeros_like(slope_ref)
-
-    @pl.when(slot == 0)
-    def _():
-        err_ref[...] = jnp.zeros_like(err_ref)
-
-    @pl.when(live_ref[slot] != 0)
-    def _():
-        u = exact(NN, py_ref[...], coeff_ref[0])
+    def work(slot, carry):
+        tile = jnp.where(slot == 0, first, last)
+        live = jnp.where(slot == 0, first < count, last > first)
+
+        @pl.when(jnp.logical_not(live))
+        def _():
+            slope_ref[slot] = jnp.zeros(slope_ref.shape[1:], F32)
+
+        @pl.when(live)
+        def _():
+            one_tile(slot, tile)
+
+        return carry
+
+    def one_tile(slot, tile):
+        u = exact(NN, py_ref[...], coeffs_ref[tile])
         u_cos, u_sin = u[:freq_y], u[freq_y:]
         px_cos, px_sin = px_ref[0], px_ref[1]
-        s_ref[0] = exact(NT, u_cos, px_cos) - exact(NT, u_sin, px_sin)
-        s_ref[1] = -(exact(NT, u_sin, px_cos) + exact(NT, u_cos, px_sin))
-        intensity[...] = jnp.zeros_like(intensity)
-
-        def forward(pair, carry):
-            spec_re, spec_im = s_ref[0], s_ref[1]
+        spec_re = exact(NT, u_cos, px_cos) - exact(NT, u_sin, px_sin)
+        spec_im = -(exact(NT, u_sin, px_cos) + exact(NT, u_cos, px_sin))
+        total = jnp.zeros((GRID_X, GRID_Y), F32)
+        for pair in range(kern // 2):
             rows = []
             for j in range(2):
                 h_re, h_im = kern_pair(2 * pair + j)
@@ -190,50 +216,48 @@
                 amp = nn(jnp.concatenate([xh, xl, xh], axis=1), wy_ref[...])
                 amps[k] = amp
                 re, im = amp[:, :LANES], amp[:, LANES:]
-                intensity[...] += weight_ref[k] * (re * re + im * im)
-            return carry
-
-        lax.fori_loop(0, kern // 2, forward, 0)
-        blurred = intensity[...]
+                total = total + weight_ref[k] * (re * re + im * im)
+        blurred = total
         for _ in range(DIFF_STEPS):
             blurred = diffuse(blurred)
         resist = 1.0 / (1.0 + jnp.exp(-RESIST_SLOPE * (blurred - RESIST_LEVEL)))
         offset = (GRID_X - CORE_X) // 2
         inner = resist[offset : offset + CORE_X]
-        misfit = inner - target_ref[0].T
-        err_ref[...] += jnp.sum(misfit * misfit, keepdims=True)
+        misfit = inner - targets_ref[tile].T
+        errors[...] += jnp.sum(misfit * misfit, keepdims=True)
         core = (2.0 * RESIST_SLOPE) * misfit * inner * (1.0 - inner)
         edge = jnp.zeros((offset, GRID_Y), F32)
         slope = jnp.concatenate([edge, core, edge], axis=0)
         for _ in range(DIFF_STEPS):
             slope = diffuse(slope)
-        intensity[...] = 2.0 * slope
-        ds_ref[...] = jnp.zeros_like(ds_ref)
-
-        def backward(k, carry):
-            gain = weight_ref[k] * intensity[...]
+        slope = 2.0 * slope
+        w_high = wy_ref[:LANES]
+        w_both = wy_ref[LANES:]
+        ds_re = jnp.zeros((freq_y, LANES), F32)
+        ds_im = jnp.zeros((freq_y, LANES), F32)
+        c_high, c_low = cs_ref[:GRID_X, :], cs_ref[GRID_X:, :]
+        for k in range(kern):
+            gain = weight_ref[k] * slope
             amp = amps[k]
             d = jnp.concatenate([gain * amp[:, :LANES], gain * amp[:, LANES:]], axis=1)
             d_high, d_low = split(d)
-            w_high = wy_ref[:LANES]
-            w_low = wy_ref[2 * LANES :]
-            dx = nt(w_high, d_high) + (nt(w_low, d_high) + nt(w_high, d_low))
+            both = nt(w_both, d_high)
+            dx = both[:LANES] + (both[LANES:] + nt(w_high, d_low))
             x_high, x_low = split(dx)
-            c_high, c_low = cs_ref[:GRID_X, :], cs_ref[GRID_X:, :]
-            df = nn(x_high, c_high) + (nn(x_high, c_low) + nn(x_low, c_high))
+            both = nn(jnp.concatenate([x_high, x_low], axis=0), c_high)
+            df = both[:LANES] + (both[LANES:] + nn(x_high, c_low))
             d_re, d_im = df[:freq_y], df[freq_y:]
             f_re = d_re[:, :LANES] + d_im[:, LANES:]
             f_im = d_im[:, :LANES] - d_re[:, LANES:]
             h_re, h_im = kern_pair(k)
-            ds_ref[0] += h_re * f_re + h_im * f_im
-            ds_ref[1] += h_re * f_im - h_im * f_re
-            return carry
-
-        lax.fori_loop(0, kern, backward, 0)
-        ds_re, ds_im = ds_ref[0], ds_ref[1]
+            ds_re = ds_re + (h_re * f_re + h_im * f_im)
+            ds_im = ds_im + (h_re * f_im - h_im * f_re)
         du_cos = exact(NN, ds_re, px_cos) - exact(NN, ds_im, px_sin)
         du_sin = -(exact(NN, ds_re, px_sin) + exact(NN, ds_im, px_cos))
-        slope_ref[0] = exact(TN, py_ref[...], jnp.concatenate([du_cos, du_sin], axis=0))
+        slope_ref[slot] = exact(TN, py_ref[...], jnp.concatenate([du_cos, du_sin], axis=0))
+
+    lax.fori_loop(0, MOST, work, 0)
+    err_ref[...] = errors[...] * (1.0 / (GRID_Y * CORE_X))
 
 
 def factors(count):
@@ -428,14 +452,6 @@
     kern, freq_y, freq_x = kernels.shape[2:]
     count = lax.axis_size("tile")
     row_fwd, row_bwd, col_tab, py, px, cs, wy = tables(tile_px, freq_y, freq_x)
-    me = lax.axis_index("tile")
-
-    mine = owner_list[:, 0] == me
-    places = jnp.arange(count, dtype=jnp.int32)
-    first = jnp.min(jnp.where(mine, places, count))
-    last = jnp.max(jnp.where(mine, places, -1))
-    ids = jnp.stack([jnp.minimum(first, count - 1), jnp.maximum(last, 0)])
-    live = jnp.stack([first < count, last > first]).astype(jnp.int32)
 
     chunk = 256
     steps = tile_px // chunk
@@ -472,38 +488,23 @@
         name="spread",
     )(pieces, target_grid.reshape(GRID_Y, CORE_X))
 
+    smem = pl.BlockSpec(memory_space=pltpu.SMEM)
+    owners = owner_list[:, 0]
     slopes, errors = pl.pallas_call(
         owner_kernel,
-        grid_spec=pltpu.PrefetchScalarGridSpec(
-            num_scalar_prefetch=3,
-            grid=(MOST,),
-            in_specs=[
-                pl.BlockSpec((1, 72, LANES), lambda s, ids, live, w: (ids[s], 0, 0)),
-                pl.BlockSpec((1, GRID_Y, CORE_X), lambda s, ids, live, w: (ids[s], 0, 0)),
-                whole((2, kern, freq_y, freq_x)),
-                whole(py.shape),
-                whole(px.shape),
-                whole(cs.shape),
-                whole(wy.shape),
-            ],
-            out_specs=[
-                pl.BlockSpec((1, 72, LANES), lambda s, *_: (s, 0, 0)),
-                whole((1, 1)),
-            ],
-            scratch_shapes=[
-                pltpu.VMEM((kern, GRID_X, 2 * GRID_Y), F32),
-                pltpu.VMEM((2, freq_y, LANES), F32),
-                pltpu.VMEM((2, freq_y, LANES), F32),
-                pltpu.VMEM((GRID_X, GRID_Y), F32),
-            ],
-        ),
+        in_specs=[smem, smem] + [vmem] * 7,
+        out_specs=[vmem, vmem],
         out_shape=[
             jax.ShapeDtypeStruct((MOST, 72, LANES), F32),
             jax.ShapeDtypeStruct((1, 1), F32),
         ],
+        scratch_shapes=[
+            pltpu.VMEM((kern, GRID_X, 2 * GRID_Y), F32),
+            pltpu.VMEM((1, 1), F32),
+        ],
         compiler_params=pltpu.CompilerParams(vmem_limit_bytes=VMEM_BYTES),
         name="owner",
-    )(ids, live, kern_weight, coeffs, targets, kernels[0], py, px, cs, wy)
+    )(owners, kern_weight, coeffs, targets, kernels[0], py, px, cs, wy)
 
     gathered = pl.pallas_call(
         functools.partial(collect_kernel, count),
@@ -516,24 +517,13 @@
         ),
         name="collect",
     )(slopes)
-    owners = owner_list[:, 0]
-    same = owners[:, None] == owners[None, :]
-    rank = jnp.sum(same & (places[None, :] < places[:, None]), axis=1).astype(jnp.int32)
-
-    def slope_of(tile):
-        inside = jnp.clip(tile, 0, count - 1)
-        flat = gathered.reshape(count * MOST, 72, LANES)
-        place = owners[inside] * MOST + rank[inside]
-        found = lax.dynamic_index_in_dim(flat, place, 0, keepdims=False)
-        return jnp.where(inside == tile, found, 0.0)
-
-    my_slopes = jnp.stack([slope_of(me), slope_of(me + 1), slope_of(me - 1)])
     out = pl.pallas_call(
         update_kernel,
         grid=(steps,),
         in_specs=[
             pl.BlockSpec((1, chunk, tile_px), lambda i: (0, i, 0)),
-            whole((3, 72, LANES)),
+            smem,
+            whole((count, MOST, 72, LANES)),
             pl.BlockSpec((chunk, 3 * ROWS), lambda i: (i, 0)),
             whole(col_tab.shape),
         ],
@@ -542,8 +532,8 @@
         scratch_shapes=[pltpu.VMEM((3 * ROWS, tile_px), BF16)],
         compiler_params=pltpu.CompilerParams(vmem_limit_bytes=VMEM_BYTES),
         name="update",
-    )(mask_tiles, my_slopes, row_bwd, col_tab)
-    return out, (errors / (GRID_Y * CORE_X)).reshape(1)
+    )(mask_tiles, owners, gathered, row_bwd, col_tab)
+    return out, errors.reshape(1)
 
 
 def solution(mesh):

time: 114 us -> 80.5 us (0.71)
  Pallas kernels: 97 us -> 79.5 us
  between operations: 9.52 us -> 0.65 us
  other arithmetic: 4.86 us -> 0 us
  local copies, waits for them, and re-layouts: 2.08 us -> 0 us
    pallas_call x1, Pallas kernels: 59.6 us -> 16.4 us  [on_device(): pl.pallas_call(functools.partial(collect_kernel, count), in_specs=[vmem],...]
    pallas_call x1, Pallas kernels: 2.99 us -> 28.3 us  [on_device(): pl.pallas_call(owner_kernel, in_specs=[smem, smem] + [vmem] * 7, out_spec...]
    dynamic_slice x2 -> x0, local copies, waits for them, and re-layouts: 2.08 us -> none  [slope_of(): place = owners[inside] * MOST + rank[inside]]
    reduce_min x1 -> x0, other arithmetic: 1.3 us -> none  [on_device(): first = jnp.min(jnp.where(mine, places, count))]
    another operation x2 -> x0, other arithmetic: 1.2 us -> none  [the longest x1 0.65 us: on_device(): my_slopes = jnp.stack([slope_of(me), slope_of(me + 1), slope_of(me - 1)])]
where the time goes in v2:
time: 80.5 us; the launch traced here: 80.1 us
  Pallas kernels  79.5 us (99%)
    pallas_call x1, Pallas kernels, on_device(): pl.pallas_call(owner_kernel, in_specs=[smem, smem] + [vmem] * 7, out_spec...  28.3 us
    pallas_call x1, Pallas kernels, on_device(): pl.pallas_call(functools.partial(spread_kernel, count), in_specs=[vmem, v...  22.4 us
    pallas_call x1, Pallas kernels, on_device(): pl.pallas_call(functools.partial(collect_kernel, count), in_specs=[vmem],...  16.4 us
    pallas_call x1, Pallas kernels, on_device(): pl.pallas_call(update_kernel, grid=(steps,), in_specs=[pl.BlockSpec((1, c...  7.02 us
    pallas_call x1, Pallas kernels, on_device(): pl.pallas_call(coeffs_kernel, grid=(steps,), in_specs=[pl.BlockSpec((1, c...  5.32 us

profile of v2, /device:TPU:0, one launch (start us, length us, event | category | flops | bytes accessed | tf_op | source)
XLA Modules:
  0.0 80.1 jit_solution(13684119025548666464)
XLA Ops:
  0.6 5.3 %coeffs.1.piece_ref = f32[3,72,128]{2,1,0:T(8,128)} custom-call(f32[1,1024,1024]{2,1,0:T(8,128)} %mask_ref.3, bf16[160,1024]{1,0:T(8,128)(2,1)} %constant.14.clone.row_ref, bf16[2,1024,384]{2,1,0:T(8,128)(2,1)} %constant.15.clone.col_ref), custom_call_target="tpu_custom_call" | custom-call | tf_op jit(solution)/shard_map/coeffs/pallas_call | solution.py:458
  5.9 22.4 %spread.1 = (f32[16,72,128]{2,1,0:T(8,128)}, f32[16,128,128]{2,1,0:T(8,128)}) custom-call(f32[3,72,128]{2,1,0:T(8,128)} %coeffs.1.piece_ref, f32[128,128]{1,0:T(8,128)} %bitcast.5), custom_call_target="tpu_custom_call" | custom-call | tf_op jit(solution)/shard_map/spread/pallas_call | solution.py:475
  28.4 28.3 %owner.1 = (f32[2,72,128]{2,1,0:T(8,128)}, f32[1,1]{1,0:T(1,128)}) custom-call(s32[16]{0:T(128)} %bitcast.6, f32[24]{0:T(128)} %weight_ref.1, f32[16,72,128]{2,1,0:T(8,128)} %get-tuple-element.6.coeffs_ref, f32[16,128,128]{2,1,0:T(8,128)} %get-tuple-element.7.targets_ref, f32[2,24,64,96]{3,2,1,0:T(8,128)} %bitcast.4, f32[128,72]{1,0:T(8,128)} %constant.16.clone.py_ref, ...), custom_call_target="tpu_custom_call" | custom-call | tf_op jit(solution)/shard_map/owner/pallas_call | solution.py:493
  56.7 16.4 %collect.1.slope_ref = f32[16,2,72,128]{3,2,1,0:T(8,128)} custom-call(f32[2,72,128]{2,1,0:T(8,128)} %get-tuple-element.8.slope_ref), custom_call_target="tpu_custom_call" | custom-call | tf_op jit(solution)/shard_map/collect/pallas_call | solution.py:509
  73.1 7.0 %update.1 = f32[1,1024,1024]{2,1,0:T(8,128)} custom-call(f32[1,1024,1024]{2,1,0:T(8,128)} %mask_ref.3, s32[16]{0:T(128)} %bitcast.7, f32[16,2,72,128]{3,2,1,0:T(8,128)} %collect.1.slope_ref, bf16[1024,240]{1,0:T(8,128)(2,1)} %constant.20.clone.row_ref, bf16[2,1024,384]{2,1,0:T(8,128)(2,1)} %constant.15.clone.col_ref), custom_call_target="tpu_custom_call" | custom-call | tf_op jit(solution)/shard_map/update/pallas_call | solution.py:520

commit v3 on v2

--- a/solution.py
+++ b/solution.py
@@ -15,6 +15,8 @@
 GRID_Y = 128
 CORE_X = 128
 MOST = 2
+PARTS = 2
+GROUP = 4
 ROWS = 80
 LANES = 128
 VMEM_BYTES = 60 << 20
@@ -117,7 +119,7 @@
 def update_kernel(mask_ref, owners_ref, slope_ref, row_ref, col_ref, out_ref, q_ref):
     @pl.when(pl.program_id(0) == 0)
     def _():
-        count = slope_ref.shape[0]
+        count = slope_ref.shape[1]
         me = lax.axis_index("tile")
 
         def slope_of(tile):
@@ -126,7 +128,7 @@
             rank = lax.fori_loop(
                 0, inside, lambda i, r: jnp.where(owners_ref[i] == owner, 1, r), jnp.int32(0)
             )
-            return jnp.where(inside == tile, slope_ref[owner, rank], 0.0)
+            return jnp.where(inside == tile, slope_ref[rank, owner], 0.0)
 
         d = jnp.concatenate([slope_of(me), slope_of(me + 1), slope_of(me - 1)], axis=1)
         d = jnp.concatenate([d, jnp.zeros((ROWS - 72, 3 * LANES), F32)], axis=0)
@@ -223,7 +225,8 @@
         resist = 1.0 / (1.0 + jnp.exp(-RESIST_SLOPE * (blurred - RESIST_LEVEL)))
         offset = (GRID_X - CORE_X) // 2
         inner = resist[offset : offset + CORE_X]
-        misfit = inner - targets_ref[tile].T
+        target = jnp.concatenate([targets_ref[part, tile] for part in range(PARTS)], axis=0)
+        misfit = inner - target.T
         errors[...] += jnp.sum(misfit * misfit, keepdims=True)
         core = (2.0 * RESIST_SLOPE) * misfit * inner * (1.0 - inner)
         edge = jnp.zeros((offset, GRID_Y), F32)
@@ -231,27 +234,29 @@
         for _ in range(DIFF_STEPS):
             slope = diffuse(slope)
         slope = 2.0 * slope
-        w_high = wy_ref[:LANES]
-        w_both = wy_ref[LANES:]
         ds_re = jnp.zeros((freq_y, LANES), F32)
         ds_im = jnp.zeros((freq_y, LANES), F32)
         c_high, c_low = cs_ref[:GRID_X, :], cs_ref[GRID_X:, :]
-        for k in range(kern):
-            gain = weight_ref[k] * slope
-            amp = amps[k]
-            d = jnp.concatenate([gain * amp[:, :LANES], gain * amp[:, LANES:]], axis=1)
-            d_high, d_low = split(d)
-            both = nt(w_both, d_high)
-            dx = both[:LANES] + (both[LANES:] + nt(w_high, d_low))
-            x_high, x_low = split(dx)
-            both = nn(jnp.concatenate([x_high, x_low], axis=0), c_high)
-            df = both[:LANES] + (both[LANES:] + nn(x_high, c_low))
-            d_re, d_im = df[:freq_y], df[freq_y:]
-            f_re = d_re[:, :LANES] + d_im[:, LANES:]
-            f_im = d_im[:, :LANES] - d_re[:, LANES:]
-            h_re, h_im = kern_pair(k)
-            ds_re = ds_re + (h_re * f_re + h_im * f_im)
-            ds_im = ds_im + (h_re * f_im - h_im * f_re)
+        for base in range(0, kern, GROUP):
+            grads = []
+            for k in range(base, base + GROUP):
+                gain = weight_ref[k] * slope
+                amp = amps[k]
+                grads.append(jnp.concatenate([gain * amp[:, :LANES], gain * amp[:, LANES:]], axis=1))
+            d_high, d_low = split(jnp.concatenate(grads, axis=0))
+            both = nt(d_high, wy_ref[LANES:])
+            dx = both[:, :LANES] + (both[:, LANES:] + nt(d_low, wy_ref[:LANES]))
+            flipped = [dx[j * GRID_X : (j + 1) * GRID_X].T for j in range(GROUP)]
+            x_high, x_low = split(jnp.concatenate(flipped, axis=0))
+            df_all = nn(x_high, c_high) + (nn(x_high, c_low) + nn(x_low, c_high))
+            for j in range(GROUP):
+                df = df_all[j * LANES : (j + 1) * LANES]
+                d_re, d_im = df[:freq_y], df[freq_y:]
+                f_re = d_re[:, :LANES] + d_im[:, LANES:]
+                f_im = d_im[:, :LANES] - d_re[:, LANES:]
+                h_re, h_im = kern_pair(base + j)
+                ds_re = ds_re + (h_re * f_re + h_im * f_im)
+                ds_im = ds_im + (h_re * f_im - h_im * f_re)
         du_cos = exact(NN, ds_re, px_cos) - exact(NN, ds_im, px_sin)
         du_sin = -(exact(NN, ds_re, px_sin) + exact(NN, ds_im, px_cos))
         slope_ref[slot] = exact(TN, py_ref[...], jnp.concatenate([du_cos, du_sin], axis=0))
@@ -367,14 +372,16 @@
 
 def spread_kernel(
     count, piece_ref, target_ref, coeff_ref, all_target_ref, near, near_send, near_recv,
-    send_c, recv_c, send_t, recv_t,
+    send_c, recv_c, *sems,
 ):
     place = Place(count)
     me = place.me
     right, left = wrapped(me + 1, count), wrapped(me - 1, count)
     coeff = Gather(place, coeff_ref, send_c, recv_c)
-    target = Gather(place, all_target_ref, send_t, recv_t)
-    all_target_ref[me] = target_ref[...]
+    targets = []
+    for part in range(PARTS):
+        targets.append(Gather(place, all_target_ref.at[part], sems[2 * part], sems[2 * part + 1]))
+        all_target_ref[part, me] = target_ref[part]
     meet([right, left] + place.partners())
     sides = []
     for side, device in ((0, right), (1, left)):
@@ -388,7 +395,8 @@
         )
         copy.start()
         sides.append(copy)
-    target.own()
+    for target in targets:
+        target.own()
     for copy in sides:
         copy.wait()
     own = piece_ref[0]
@@ -396,23 +404,33 @@
     own = own + jnp.where(me < count - 1, near[1], 0.0)
     coeff_ref[me] = own
     coeff.own()
-    target.outer_arrivals()
-    coeff.outer_arrivals()
-    target.inner_arrivals()
-    coeff.inner_arrivals()
-    target.finish()
-    coeff.finish()
-
-
-def collect_kernel(count, slope_ref, all_ref, send, recv):
+    forward(targets + [coeff])
+
+
+def collect_kernel(count, slope_ref, all_ref, *sems):
     place = Place(count)
-    gather = Gather(place, all_ref, send, recv)
-    all_ref[place.me] = slope_ref[...]
+    gathers = [
+        Gather(place, all_ref.at[slot], sems[2 * slot], sems[2 * slot + 1]) for slot in range(MOST)
+    ]
+    for slot in range(MOST):
+        all_ref[slot, place.me] = slope_ref[slot]
     meet(place.partners())
-    gather.own()
-    gather.outer_arrivals()
-    gather.inner_arrivals()
-    gather.finish()
+    together(gathers)
+
+
+def together(gathers):
+    for gather in gathers:
+        gather.own()
+    forward(gathers)
+
+
+def forward(gathers):
+    for gather in gathers:
+        gather.outer_arrivals()
+    for gather in gathers:
+        gather.inner_arrivals()
+    for gather in gathers:
+        gather.finish()
 
 
 def tables(tile_px, freq_y, freq_x):
@@ -478,15 +496,15 @@
         out_specs=[vmem, vmem],
         out_shape=[
             jax.ShapeDtypeStruct((count, 72, LANES), F32),
-            jax.ShapeDtypeStruct((count, GRID_Y, CORE_X), F32),
+            jax.ShapeDtypeStruct((PARTS, count, GRID_Y // PARTS, CORE_X), F32),
         ],
         scratch_shapes=[pltpu.VMEM((2, 72, LANES), F32), dma((2,)), dma((2,))]
-        + [dma((count,))] * 4,
+        + [dma((count,))] * (2 + 2 * PARTS),
         compiler_params=pltpu.CompilerParams(
             collective_id=0, has_side_effects=True, vmem_limit_bytes=VMEM_BYTES
         ),
         name="spread",
-    )(pieces, target_grid.reshape(GRID_Y, CORE_X))
+    )(pieces, target_grid.reshape(PARTS, GRID_Y // PARTS, CORE_X))
 
     smem = pl.BlockSpec(memory_space=pltpu.SMEM)
     owners = owner_list[:, 0]
@@ -510,8 +528,8 @@
         functools.partial(collect_kernel, count),
         in_specs=[vmem],
         out_specs=vmem,
-        out_shape=jax.ShapeDtypeStruct((count, MOST, 72, LANES), F32),
-        scratch_shapes=[dma((count,))] * 2,
+        out_shape=jax.ShapeDtypeStruct((MOST, count, 72, LANES), F32),
+        scratch_shapes=[dma((count,))] * (2 * MOST),
         compiler_params=pltpu.CompilerParams(
             collective_id=1, has_side_effects=True, vmem_limit_bytes=VMEM_BYTES
         ),
@@ -523,7 +541,7 @@
         in_specs=[
             pl.BlockSpec((1, chunk, tile_px), lambda i: (0, i, 0)),
             smem,
-            whole((count, MOST, 72, LANES)),
+            whole((MOST, count, 72, LANES)),
             pl.BlockSpec((chunk, 3 * ROWS), lambda i: (i, 0)),
             whole(col_tab.shape),
         ],

time: 80.5 us -> 72.9 us (0.906)
  Pallas kernels: 79.5 us -> 71.3 us
    pallas_call x1, Pallas kernels: 28.3 us -> 12.2 us  [on_device(): pl.pallas_call(owner_kernel, in_specs=[smem, smem] + [vmem] * 7, out_spec...]
    pallas_call x1, Pallas kernels: 16.4 us -> 23.4 us  [on_device(): pl.pallas_call(functools.partial(collect_kernel, count), in_specs=[vmem],...]
    pallas_call x1, Pallas kernels: 22.4 us -> 23.4 us  [on_device(): pl.pallas_call(functools.partial(spread_kernel, count), in_specs=[vmem, v...]
where the time goes in v3:
time: 72.9 us; the launch traced here: 72 us
  Pallas kernels  71.3 us (98%)
    pallas_call x1, Pallas kernels, on_device(): pl.pallas_call(functools.partial(spread_kernel, count), in_specs=[vmem, v...  23.4 us
    pallas_call x1, Pallas kernels, on_device(): pl.pallas_call(functools.partial(collect_kernel, count), in_specs=[vmem],...  23.4 us
    pallas_call x1, Pallas kernels, on_device(): pl.pallas_call(owner_kernel, in_specs=[smem, smem] + [vmem] * 7, out_spec...  12.2 us
    pallas_call x1, Pallas kernels, on_device(): pl.pallas_call(update_kernel, grid=(steps,), in_specs=[pl.BlockSpec((1, c...  7.01 us
    pallas_call x1, Pallas kernels, on_device(): pl.pallas_call(coeffs_kernel, grid=(steps,), in_specs=[pl.BlockSpec((1, c...  5.32 us

profile of v3, /device:TPU:0, one launch (start us, length us, event | category | flops | bytes accessed | tf_op | source)
XLA Modules:
  0.0 72.0 jit_solution(14973835947649474148)
XLA Ops:
  0.6 5.3 %coeffs.1.piece_ref = f32[3,72,128]{2,1,0:T(8,128)} custom-call(f32[1,1024,1024]{2,1,0:T(8,128)} %mask_ref.3, bf16[160,1024]{1,0:T(8,128)(2,1)} %constant.14.clone.row_ref, bf16[2,1024,384]{2,1,0:T(8,128)(2,1)} %constant.15.clone.col_ref), custom_call_target="tpu_custom_call" | custom-call | tf_op jit(solution)/shard_map/coeffs/pallas_call | solution.py:476
  5.9 23.4 %spread.1 = (f32[16,72,128]{2,1,0:T(8,128)}, f32[2,16,64,128]{3,2,1,0:T(8,128)}) custom-call(f32[3,72,128]{2,1,0:T(8,128)} %coeffs.1.piece_ref, f32[2,64,128]{2,1,0:T(8,128)} %bitcast.5), custom_call_target="tpu_custom_call" | custom-call | tf_op jit(solution)/shard_map/spread/pallas_call | solution.py:493
  29.4 12.2 %owner.1 = (f32[2,72,128]{2,1,0:T(8,128)}, f32[1,1]{1,0:T(1,128)}) custom-call(s32[16]{0:T(128)} %bitcast.6, f32[24]{0:T(128)} %weight_ref.1, f32[16,72,128]{2,1,0:T(8,128)} %get-tuple-element.6.coeffs_ref, f32[2,16,64,128]{3,2,1,0:T(8,128)} %get-tuple-element.7.targets_ref, f32[2,24,64,96]{3,2,1,0:T(8,128)} %bitcast.4, f32[128,72]{1,0:T(8,128)} %constant.16.clone.py_ref, ...), custom_call_target="tpu_custom_call" | custom-call | tf_op jit(solution)/shard_map/owner/pallas_call | solution.py:511
  41.5 23.4 %collect.1.slope_ref = f32[2,16,72,128]{3,2,1,0:T(8,128)} custom-call(f32[2,72,128]{2,1,0:T(8,128)} %get-tuple-element.8.slope_ref), custom_call_target="tpu_custom_call" | custom-call | tf_op jit(solution)/shard_map/collect/pallas_call | solution.py:527
  64.9 7.0 %update.1 = f32[1,1024,1024]{2,1,0:T(8,128)} custom-call(f32[1,1024,1024]{2,1,0:T(8,128)} %mask_ref.3, s32[16]{0:T(128)} %bitcast.7, f32[2,16,72,128]{3,2,1,0:T(8,128)} %collect.1.slope_ref, bf16[1024,240]{1,0:T(8,128)(2,1)} %constant.20.clone.row_ref, bf16[2,1024,384]{2,1,0:T(8,128)(2,1)} %constant.15.clone.col_ref), custom_call_target="tpu_custom_call" | custom-call | tf_op jit(solution)/shard_map/update/pallas_call | solution.py:538

commit v4 on v3

--- a/solution.py
+++ b/solution.py
@@ -199,26 +199,25 @@
         spec_re = exact(NT, u_cos, px_cos) - exact(NT, u_sin, px_sin)
         spec_im = -(exact(NT, u_sin, px_cos) + exact(NT, u_cos, px_sin))
         total = jnp.zeros((GRID_X, GRID_Y), F32)
-        for pair in range(kern // 2):
+        c_high, c_low = cs_ref[:GRID_X, :], cs_ref[GRID_X:, :]
+        for base in range(0, kern, GROUP):
             rows = []
-            for j in range(2):
-                h_re, h_im = kern_pair(2 * pair + j)
+            for k in range(base, base + GROUP):
+                h_re, h_im = kern_pair(k)
                 f_re = h_re * spec_re - h_im * spec_im
                 f_im = h_re * spec_im + h_im * spec_re
                 rows.append(jnp.concatenate([f_re, -f_im], axis=1))
                 rows.append(jnp.concatenate([f_im, f_re], axis=1))
             f_high, f_low = split(jnp.concatenate(rows, axis=0))
-            both = nt(cs_ref[...], f_high)
-            x = both[:GRID_X] + (both[GRID_X:] + nt(cs_ref[:GRID_X, :], f_low))
-            x_high, x_low = split(x)
-            for j in range(2):
-                k = 2 * pair + j
-                part = slice(j * LANES, (j + 1) * LANES)
-                xh, xl = x_high[:, part], x_low[:, part]
-                amp = nn(jnp.concatenate([xh, xl, xh], axis=1), wy_ref[...])
-                amps[k] = amp
+            x_all = nt(f_high, c_high) + (nt(f_high, c_low) + nt(f_low, c_high))
+            flipped = [x_all[j * LANES : (j + 1) * LANES].T for j in range(GROUP)]
+            x_high, x_low = split(jnp.concatenate(flipped, axis=0))
+            amp_all = nn(jnp.concatenate([x_high, x_low, x_high], axis=1), wy_ref[...])
+            for j in range(GROUP):
+                amp = amp_all[j * GRID_X : (j + 1) * GRID_X]
+                amps[base + j] = amp
                 re, im = amp[:, :LANES], amp[:, LANES:]
-                total = total + weight_ref[k] * (re * re + im * im)
+                total = total + weight_ref[base + j] * (re * re + im * im)
         blurred = total
         for _ in range(DIFF_STEPS):
             blurred = diffuse(blurred)
@@ -236,7 +235,6 @@
         slope = 2.0 * slope
         ds_re = jnp.zeros((freq_y, LANES), F32)
         ds_im = jnp.zeros((freq_y, LANES), F32)
-        c_high, c_low = cs_ref[:GRID_X, :], cs_ref[GRID_X:, :]
         for base in range(0, kern, GROUP):
             grads = []
             for k in range(base, base + GROUP):

time: 72.9 us -> 71.1 us (0.975); the launches traced: 72 us -> 70.9 us
  Pallas kernels: 71.3 us -> 70.3 us
    pallas_call x1, Pallas kernels: 12.2 us -> 2.86 us  [on_device(): pl.pallas_call(owner_kernel, in_specs=[smem, smem] + [vmem] * 7, out_spec...]
    pallas_call x1, Pallas kernels: 23.4 us -> 31.7 us  [on_device(): pl.pallas_call(functools.partial(collect_kernel, count), in_specs=[vmem],...]
where the time goes in v4:
time: 71.1 us; the launch traced here: 70.9 us
  Pallas kernels  70.3 us (99%)
    pallas_call x1, Pallas kernels, on_device(): pl.pallas_call(functools.partial(collect_kernel, count), in_specs=[vmem],...  31.7 us
    pallas_call x1, Pallas kernels, on_device(): pl.pallas_call(functools.partial(spread_kernel, count), in_specs=[vmem, v...  23.4 us
    pallas_call x1, Pallas kernels, on_device(): pl.pallas_call(update_kernel, grid=(steps,), in_specs=[pl.BlockSpec((1, c...  7.02 us
    pallas_call x1, Pallas kernels, on_device(): pl.pallas_call(coeffs_kernel, grid=(steps,), in_specs=[pl.BlockSpec((1, c...  5.32 us
    pallas_call x1, Pallas kernels, on_device(): pl.pallas_call(owner_kernel, in_specs=[smem, smem] + [vmem] * 7, out_spec...  2.86 us

profile of v4, /device:TPU:0, one launch (start us, length us, event | category | flops | bytes accessed | tf_op | source)
XLA Modules:
  0.0 70.9 jit_solution(1942848942101407938)
XLA Ops:
  0.6 5.3 %coeffs.1.piece_ref = f32[3,72,128]{2,1,0:T(8,128)} custom-call(f32[1,1024,1024]{2,1,0:T(8,128)} %mask_ref.3, bf16[160,1024]{1,0:T(8,128)(2,1)} %constant.14.clone.row_ref, bf16[2,1024,384]{2,1,0:T(8,128)(2,1)} %constant.15.clone.col_ref), custom_call_target="tpu_custom_call" | custom-call | tf_op jit(solution)/shard_map/coeffs/pallas_call | solution.py:474
  5.9 23.4 %spread.1 = (f32[16,72,128]{2,1,0:T(8,128)}, f32[2,16,64,128]{3,2,1,0:T(8,128)}) custom-call(f32[3,72,128]{2,1,0:T(8,128)} %coeffs.1.piece_ref, f32[2,64,128]{2,1,0:T(8,128)} %bitcast.5), custom_call_target="tpu_custom_call" | custom-call | tf_op jit(solution)/shard_map/spread/pallas_call | solution.py:491
  29.4 2.9 %owner.1 = (f32[2,72,128]{2,1,0:T(8,128)}, f32[1,1]{1,0:T(1,128)}) custom-call(s32[16]{0:T(128)} %bitcast.6, f32[24]{0:T(128)} %weight_ref.1, f32[16,72,128]{2,1,0:T(8,128)} %get-tuple-element.6.coeffs_ref, f32[2,16,64,128]{3,2,1,0:T(8,128)} %get-tuple-element.7.targets_ref, f32[2,24,64,96]{3,2,1,0:T(8,128)} %bitcast.4, f32[128,72]{1,0:T(8,128)} %constant.16.clone.py_ref, ...), custom_call_target="tpu_custom_call" | custom-call | tf_op jit(solution)/shard_map/owner/pallas_call | solution.py:509
  32.2 31.7 %collect.1.slope_ref = f32[2,16,72,128]{3,2,1,0:T(8,128)} custom-call(f32[2,72,128]{2,1,0:T(8,128)} %get-tuple-element.8.slope_ref), custom_call_target="tpu_custom_call" | custom-call | tf_op jit(solution)/shard_map/collect/pallas_call | solution.py:525
  63.9 7.0 %update.1 = f32[1,1024,1024]{2,1,0:T(8,128)} custom-call(f32[1,1024,1024]{2,1,0:T(8,128)} %mask_ref.3, s32[16]{0:T(128)} %bitcast.7, f32[2,16,72,128]{3,2,1,0:T(8,128)} %collect.1.slope_ref, bf16[1024,240]{1,0:T(8,128)(2,1)} %constant.20.clone.row_ref, bf16[2,1024,384]{2,1,0:T(8,128)(2,1)} %constant.15.clone.col_ref), custom_call_target="tpu_custom_call" | custom-call | tf_op jit(solution)/shard_map/update/pallas_call | solution.py:536
